TPU v7x, 32 devices: a whole 2x2x4 slice. The times are simulated.
32 devices in a mesh: bx: 4 (over y, core), by: 8 (over z, x).
Axes of the slice: x: 2, y: 2, z: 4, core: 2. Of those that a mesh axis runs over, the one named last changes fastest.
Arguments:
- solution: float32 [4, 2048, 2048], P(None, 'by', 'bx'), may hold values from -6 to 6
- source: float32 [4, 2048, 2048], P(None, 'by', 'bx'), may hold values from -12 to 12
- class_ids: int32 [4, 2048, 2048], P(None, 'by', 'bx'), may hold values from 0 to 7
- conductivity: float32 [8], replicated, may hold values from 0.3 to 3
- spacing_x: float32 [2048], P('bx'), may hold values from 0.7 to 1.4
- spacing_y: float32 [2048], P('by'), may hold values from 0.7 to 1.4
- spacing_z: float32 [4], replicated, may hold values from 0.7 to 1.4
- forward_x: bfloat16 [2048, 2048], P('bx'), may hold values from -0.125 to 0.125
- forward_y: bfloat16 [2048, 2048], P('by'), may hold values from -0.125 to 0.125
- forward_z: bfloat16 [4, 4], replicated, may hold values from -3 to 3
- inverse_x: bfloat16 [2048, 2048], P('bx'), may hold values from -0.125 to 0.125
- inverse_y: bfloat16 [2048, 2048], P('by'), may hold values from -0.125 to 0.125
- inverse_z: bfloat16 [4, 4], replicated, may hold values from -3 to 3
- eigen_x: float32 [2048], P('bx'), may hold values from 0.05 to 4
- eigen_y: float32 [2048], P('by'), may hold values from 0.05 to 4
- eigen_z: float32 [4], replicated, may hold values from 0.05 to 4
Outputs:
- corrected: float32 [4, 2048, 2048], P(None, 'by', 'bx')
All inputs are finite; a program needn't handle non-finite values.
Results may differ from a plain program's by a relative error of at most 0.0039.
Values may be sent and summed in bfloat16 or wider, within the bound.
No kernel may reach another device: no remote copies, remote signals or barrier semaphores. Data moves between devices by JAX's collectives and lax.ppermute only.
A program may use at most 64 MiB of HBM per device.

v0:
```python
import jax
import jax.numpy as jnp
from jax import lax
from jax.sharding import PartitionSpec as P

CLASSES = 8


shift_value = 0.1


def extended(value, sides, width):
    for axis, dim in sides:
        size, length = (lax.axis_size(axis), value.shape[dim])
        up = [(i, (i + 1) % size) for i in range(size - 1)]
        down = [(j, i) for i, j in up]
        last = lax.slice_in_dim(value, length - width, length, axis=dim)
        first = lax.slice_in_dim(value, 0, width, axis=dim)
        before = lax.ppermute(last, axis, up)
        after = lax.ppermute(first, axis, down)
        value = jnp.concatenate([before, value, after], axis=dim)
    return value


def coefficients(class_ids, conductivity):
    result = jnp.zeros(class_ids.shape, jnp.float32)
    for index in range(CLASSES):
        result = result + jnp.where(class_ids == index, conductivity[index], jnp.float32(0.0))
    return result


def operate(solution, coef):
    stacked = jnp.stack([solution, coef])
    padded = extended(stacked, (("bx", 3), ("by", 2)), 1)
    padded = jnp.pad(padded, ((0, 0), (1, 1), (0, 0), (0, 0)))
    values = padded[0]
    padcoef = padded[1]
    slices = [
        (slice(2, None), slice(1, -1), slice(1, -1)),
        (slice(0, -2), slice(1, -1), slice(1, -1)),
        (slice(1, -1), slice(2, None), slice(1, -1)),
        (slice(1, -1), slice(0, -2), slice(1, -1)),
        (slice(1, -1), slice(1, -1), slice(2, None)),
        (slice(1, -1), slice(1, -1), slice(0, -2)),
    ]
    result = jnp.zeros(solution.shape, jnp.float32)
    for where_at in slices:
        neighbour = values[where_at]
        ncoef = padcoef[where_at]
        face = jnp.where(ncoef > 0, 2.0 * coef * ncoef / (coef + ncoef), coef)
        result = result + face * (solution - neighbour)
    return result


def x_high(values, matrix_rows):
    columns = matrix_rows.astype(jnp.float32)
    return jnp.einsum(
        "kjx,mx->kjm",
        lax.all_gather(values, "bx", axis=2, tiled=True),
        columns,
        precision=lax.Precision.HIGHEST,
    )


def y_low(values, matrix_rows):
    return jnp.einsum(
        "kjm,nj->knm",
        lax.all_gather(values, "by", axis=1, tiled=True),
        matrix_rows,
        preferred_element_type=jnp.float32,
    )


def on_device(
    solution,
    source,
    class_ids,
    conductivity,
    spacing_x,
    spacing_y,
    spacing_z,
    forward_x,
    forward_y,
    forward_z,
    inverse_x,
    inverse_y,
    inverse_z,
    eigen_x,
    eigen_y,
    eigen_z,
):
    highest = lax.Precision.HIGHEST
    coef = coefficients(class_ids, conductivity)
    operated = operate(solution, coef)
    weights = spacing_z[:, None, None] * spacing_y[None, :, None] * spacing_x[None, None, :]
    restricted = (weights * (source - operated)).astype(jnp.bfloat16)
    modes_xy = x_high(y_low(restricted, forward_y), forward_x)
    modes = jnp.einsum("qk,knm->qnm", forward_z.astype(jnp.float32), modes_xy, precision=highest)
    divisor = eigen_x[None, None, :] + eigen_y[None, :, None] + eigen_z[:, None, None] + shift_value
    scaled = modes / divisor
    spectral = jnp.einsum(
        "kq,qnm->knm", inverse_z.astype(jnp.float32), scaled, precision=highest
    ).astype(jnp.bfloat16)
    field = x_high(y_low(spectral, inverse_y), inverse_x)
    return solution + weights * field


def solution(mesh):
    in_specs = (
        P(None, "by", "bx"),
        P(None, "by", "bx"),
        P(None, "by", "bx"),
        P(),
        P("bx"),
        P("by"),
        P(),
        P("bx", None),
        P("by", None),
        P(),
        P("bx", None),
        P("by", None),
        P(),
        P("bx"),
        P("by"),
        P(),
    )
    out_specs = P(None, "by", "bx")
    return jax.shard_map(
        on_device, mesh=mesh, in_specs=in_specs, out_specs=out_specs, check_vma=False
    )
```

profile of v0, /device:TPU:0, one launch (start us, length us, event | category | flops | bytes accessed | tf_op | source)
XLA Modules:
  0.0 509.1 jit_solution(13231729642086671290)
XLA Ops:
  6.5 0.0 copy-start
  6.5 0.0 all-gather.5.cloned.1.call-start
  6.5 1.6 fusion.49
  8.1 2.9 copy.49
  11.0 2.9 copy.77
  13.9 0.0 copy-start.1
  13.9 8.2 %fusion.47 = f32[1,4,256,512]{2,3,1,0:T(8,128)S(1)} fusion(f32[]{:T(128)} %bitcast.8, s32[4,256,512]{1,2,0:T(8,128)} %copy.49, f32[]{:T(128)} %bitcast.7, f32[]{:T(128)} %bitcast.6, f32[]{:T(128)} %bitcast.5, f32[]{:T(128)} %bitcast.4, f32[]{:T(128)} %bitcast.3, f32[]{:T(128)} %bitcast.2, f32[]{:T(128)} %bitcast.1), kind=kLoop, calls=%fused_computation.72 | loop fusion | flops 12058624 | bytes 4194336 | tf_op jit(solution)/shard_map/stack | solution.py:33
  22.1 0.0 copy-start.3
  22.1 0.0 copy-done.1
  22.1 2.4 collective-permute-start
  24.5 1.3 collective-permute-start.1
  25.8 0.0 collective-permute-done
  25.8 3.9 collective-permute-done.1
  29.7 0.0 copy-done.3
  29.7 0.4 pad_maximum_fusion
  30.1 2.6 fusion.48
  32.8 0.0 copy-start.9
  32.8 0.0 copy-start.10
  32.8 2.4 copy.61
  35.2 3.4 collective-permute-start.2
  38.6 2.4 copy.62
  40.9 1.3 collective-permute-start.3
  42.2 0.0 copy-done.9
  42.2 0.0 copy-done.10
  42.2 0.1 broadcast_multiply_fusion
  42.3 2.9 copy.71
  45.2 0.0 collective-permute-done.2
  45.3 2.1 copy.63
  47.3 0.0 collective-permute-done.3
  47.3 2.0 copy.64
  49.3 10.3 %select_maximum_fusion = f32[2,6,258,514]{2,3,1,0:T(8,128)} fusion(f32[2,4,1,514]{2,3,1,0:T(8,128)} %copy.64, f32[2,4,1,514]{2,3,1,0:T(8,128)} %copy.63, f32[2,4,256,1]{2,3,1,0:T(1,128)S(1)} %copy.60, f32[2,4,256,1]{2,3,1,0:T(1,128)S(1)} %copy.59, f32[1,4,256,512]{2,3,1,0:T(8,128)} %copy-done.3, f32[1,4,256,512]{2,3,1,0:T(8,128)} %bitcast.51), kind=kLoop, calls=%fused_computation.2 | loop fusion | flops 22278816 | bytes 10608960 | tf_op jit(solution)/shard_map/concatenate | solution.py:21
  59.6 4.6 slice_bitcast_fusion.1
  64.2 0.0 copy-done.2
  64.2 0.4 copy-done.4
  64.7 0.0 copy-done.6
  64.7 16.4 %fusion.3 = bf16[4,256,512]{1,2,0:T(8,128)(2,1)} fusion(f32[4,256,512]{1,2,0:T(8,128)} %copy.71, f32[4,256,512]{1,2,0:T(8,128)S(1)} %copy-done.2, f32[6,258,514]{1,2,0:T(8,128)S(1)} %get-tuple-element.6, f32[6,258,514]{1,2,0:T(8,128)S(1)} %get-tuple-element.5, f32[512]{0:T(512)S(1)} %copy-done.6, f32[4,256]{1,0:T(4,128)S(1)} %broadcast_multiply_fusion, ...), kind=kLoop, calls=%fused_computation.15 | loop fusion | flops 39321600 | bytes 32512032 | tf_op jit(solution)/shard_map/convert_element_type | solution.py:96
  81.1 0.0 all-gather.5.cloned.1.call-update
  81.1 0.2 all-gather.7.cloned.1.call-start
  81.4 128.5 %all-gather.5.cloned.1.call-done = bf16[4,2048,512]{1,2,0:T(8,128)(2,1)} async-done(((bf16[4,256,512]{1,2,0:T(8,128)(2,1)}), bf16[4,2048,512]{1,2,0:T(8,128)(2,1)}) %all-gather.5.cloned.1.call-update) | async-done | bytes 8388624 | tf_op jit(solution)/shard_map/all_gather | solution.py:68
  209.9 7.4 %convolution_bitcast_fusion = f32[4,256,512]{1,2,0:T(8,128)} fusion(bf16[4,2048,512]{1,2,0:T(8,128)(2,1)} %all-gather.5.cloned.1.call-done, bf16[256,2048]{1,0:T(8,128)(2,1)} %param.24), kind=kOutput, calls=%fused_computation.57 | convolution fusion | flops 2147483648 | bytes 11534336 | tf_op jit(solution)/shard_map/kjm,nj->knm/dot_general | solution.py:66
  217.2 0.0 all-gather.7.cloned.1.call-update
  217.3 0.0 all-gather.9.cloned.1.call-start
  217.3 0.6 copy-done.5
  217.9 0.0 copy-done.7
  217.9 0.1 broadcast_add_fusion
  218.0 0.0 copy-start.8
  218.1 55.8 %all-gather.7.cloned.1.call-done = f32[4,256,2048]{1,2,0:T(8,128)} async-done(((f32[4,256,512]{1,2,0:T(8,128)}), f32[4,256,2048]{1,2,0:T(8,128)}) %all-gather.7.cloned.1.call-update) | async-done | bytes 8388624 | tf_op jit(solution)/shard_map/all_gather | solution.py:59
  273.9 0.0 copy-done
  273.9 15.9 %fusion.19 = f32[4,256,512]{2,1,0:T(8,128)S(1)} fusion(f32[4,256,2048]{1,2,0:T(8,128)} %all-gather.7.cloned.1.call-done, bf16[512,2048]{1,0:T(8,128)(2,1)S(1)} %copy-done), kind=kOutput, calls=%fused_computation.38 | convolution fusion | flops 12884901888 | bytes 12582912 | tf_op jit(solution)/shard_map/kjx,mx->kjm/dot_general | solution.py:57
  289.8 0.0 copy-done.8
  289.8 0.0 copy-start.11
  289.8 0.0 copy-start.12
  289.8 3.2 fusion.21
  293.0 0.0 copy-done.11
  293.1 0.0 copy-done.12
  293.1 3.9 fusion.38
  297.0 0.0 all-gather.9.cloned.1.call-update
  297.0 0.0 all-gather.11.cloned.1.call-start
  297.1 125.0 %all-gather.9.cloned.1.call-done = bf16[4,2048,512]{2,0,1:T(4,128)(2,1)} async-done(((bf16[4,256,512]{2,0,1:T(4,128)(2,1)}), bf16[4,2048,512]{2,0,1:T(4,128)(2,1)}) %all-gather.9.cloned.1.call-update) | async-done | bytes 8388624 | tf_op jit(solution)/shard_map/all_gather | solution.py:68
  422.1 9.6 %fusion.32 = f32[4,256,512]{1,2,0:T(8,128)} fusion(bf16[4,2048,512]{2,0,1:T(4,128)(2,1)} %all-gather.9.cloned.1.call-done, bf16[256,2048]{1,0:T(8,128)(2,1)} %param.27), kind=kOutput, calls=%fused_computation.56 | convolution fusion | flops 2147483648 | bytes 11534336 | tf_op jit(solution)/shard_map/kjm,nj->knm/dot_general | solution.py:66
  431.7 0.0 all-gather.11.cloned.1.call-update
  431.7 56.6 %all-gather.11.cloned.1.call-done = f32[4,256,2048]{1,2,0:T(8,128)} async-done(((f32[4,256,512]{1,2,0:T(8,128)}), f32[4,256,2048]{1,2,0:T(8,128)}) %all-gather.11.cloned.1.call-update) | async-done | bytes 8388624 | tf_op jit(solution)/shard_map/all_gather | solution.py:59
  488.4 11.3 %fusion.4 = f32[4,256,512]{1,2,0:T(8,128)} fusion(f32[4,256,512]{1,2,0:T(8,128)} %copy.77, f32[4,256,2048]{1,2,0:T(8,128)} %all-gather.11.cloned.1.call-done, bf16[512,2048]{1,0:T(8,128)(2,1)} %param.26, f32[512]{0:T(512)S(1)} %copy-done.6, f32[4,256]{1,0:T(4,128)S(1)} %broadcast_multiply_fusion), kind=kOutput, calls=%fused_computation.16 | convolution fusion | flops 12886474752 | bytes 14686208 | tf_op jit(solution)/shard_map/kjx,mx->kjm/dot_general | solution.py:57
  499.7 2.9 copy.78
  (10 shorter events, 0.0 us)
Async XLA Ops:
  6.5 267.4 %copy-start = (bf16[512,2048]{1,0:T(8,128)(2,1)S(1)}, bf16[512,2048]{1,0:T(8,128)(2,1)}, u32[]{:S(2)}) copy-start(bf16[512,2048]{1,0:T(8,128)(2,1)} %param.23) | copy-start | bytes 6291460
  6.5 203.3 %all-gather.5.cloned.1.call-start = ((), (), s32[]{:S(2)}) async-start(), calls=%async_computation | async-start | bytes 9437184 | tf_op jit(solution)/shard_map/all_gather | solution.py:68
  13.9 8.2 %copy-start.1 = (f32[4,256,512]{1,2,0:T(8,128)S(1)}, f32[4,256,512]{1,2,0:T(8,128)}, u32[]{:S(2)}) copy-start(f32[4,256,512]{1,2,0:T(8,128)} %copy.77) | copy-start | bytes 6291460
  22.1 7.6 %copy-start.3 = (f32[1,4,256,512]{2,3,1,0:T(8,128)}, f32[1,4,256,512]{2,3,1,0:T(8,128)S(1)}, u32[]{:S(2)}) copy-start(f32[1,4,256,512]{2,3,1,0:T(8,128)S(1)} %fusion.47) | copy-start | bytes 6291460
  22.1 3.7 collective-permute-start
  24.5 5.2 %collective-permute-start.1 = (f32[2,4,256,1]{2,1,3,0:T(4,128)S(1)}, f32[2,4,256,1]{2,1,3,0:T(4,128)S(1)}, u32[]{:S(2)}, u32[]{:S(2)}) collective-permute-start(f32[2,4,256,1]{2,1,3,0:T(4,128)S(1)} %copy.58), channel_id=1, source_target_pairs={{8,0},{16,8},{24,16},{9,1},{17,9},{25,17},{10,2},{18,10},{26,18},{... | collective-permute-start | bytes 24584 | tf_op jit(solution)/shard_map/ppermute | solution.py:20
  32.8 9.5 %copy-start.9 = (f32[256]{0:T(256)S(1)}, f32[256]{0:T(256)}, u32[]{:S(2)}) copy-start(f32[256]{0:T(256)} %param.21) | copy-start | bytes 3076
  32.8 9.5 %copy-start.10 = (f32[4]{0:T(128)S(1)}, f32[4]{0:T(128)}, u32[]{:S(2)}) copy-start(f32[4]{0:T(128)} %param.22) | copy-start | bytes 52
  35.2 10.1 %collective-permute-start.2 = (f32[2,4,1,514]{3,1,2,0:T(4,128)S(1)}, f32[2,4,1,514]{3,1,2,0:T(4,128)S(1)}, u32[]{:S(2)}, u32[]{:S(2)}) collective-permute-start(f32[2,4,1,514]{3,1,2,0:T(4,128)S(1)} %copy.61), channel_id=1, source_target_pairs={{0,1},{1,2},{2,3},{3,4},{4,5},{5,6},{6,7},{8,9},{9,10},{10,11},{11... | collective-permute-start | bytes 49352 | tf_op jit(solution)/shard_map/ppermute | solution.py:19
  40.9 6.4 %collective-permute-start.3 = (f32[2,4,1,514]{3,1,2,0:T(4,128)S(1)}, f32[2,4,1,514]{3,1,2,0:T(4,128)S(1)}, u32[]{:S(2)}, u32[]{:S(2)}) collective-permute-start(f32[2,4,1,514]{3,1,2,0:T(4,128)S(1)} %copy.62), channel_id=1, source_target_pairs={{1,0},{2,1},{3,2},{4,3},{5,4},{6,5},{7,6},{9,8},{10,9},{11,10},{12... | collective-permute-start | bytes 49352 | tf_op jit(solution)/shard_map/ppermute | solution.py:20
  59.6 4.6 copy-start.2
  59.6 5.0 copy-start.4
  59.6 5.0 copy-start.6
  81.1 192.8 %all-gather.7.cloned.1.call-start = ((), (), s32[]{:S(2)}) async-start(), calls=%async_computation.1 | async-start | bytes 10485760 | tf_op jit(solution)/shard_map/all_gather | solution.py:59
  217.2 0.7 copy-start.5
  217.2 0.7 copy-start.7
  217.3 204.8 %all-gather.9.cloned.1.call-start = ((), (), s32[]{:S(2)}) async-start(), calls=%async_computation.2 | async-start | bytes 9437184 | tf_op jit(solution)/shard_map/all_gather | solution.py:68
  218.0 71.7 %copy-start.8 = (bf16[4,4]{1,0:T(4,128)(2,1)S(1)}, bf16[4,4]{1,0:T(4,128)(2,1)}, u32[]{:S(2)}) copy-start(bf16[4,4]{1,0:T(4,128)(2,1)} %param.25) | copy-start | bytes 100
  289.8 3.3 copy-start.11
  289.8 3.3 copy-start.12
  297.0 191.3 %all-gather.11.cloned.1.call-start = ((), (), s32[]{:S(2)}) async-start(), calls=%async_computation.3 | async-start | bytes 10485760 | tf_op jit(solution)/shard_map/all_gather | solution.py:59
Sparse Core Ops, SparseCore 0:
  81.2 128.5 all-gather.4
  217.4 56.4 all-gather.6
  297.1 124.9 all-gather.8
  431.9 56.4 all-gather.10
where the time goes:
time: 510 us; the launch traced here: 509 us
  waiting for transfers between devices  370 us (73%)
  matrix products  51.3 us (10%)
  other arithmetic  35.5 us (7%)
  local copies, waits for them, and re-layouts  30.3 us (6%)
  between operations  13.4 us (3%)
  starting transfers between devices  8.65 us (2%)
    all_gather x2, waiting for transfers between devices, y_low(): lax.all_gather(values, 'by', axis=1, tiled=True)  254 us
    all_gather x2, waiting for transfers between devices, x_high(): lax.all_gather(values, 'bx', axis=2, tiled=True)  112 us
    dot_general x2, matrix products, x_high(): jnp.einsum('kjx,mx->kjm', lax.all_gather(values, 'bx', axis=2, tiled=True...  27.2 us
    dot_general x2, matrix products, y_low(): jnp.einsum('kjm,nj->knm', lax.all_gather(values, 'by', axis=1, tiled=True...  17 us
    convert_element_type x1, other arithmetic, on_device(): restricted = (weights * (source - operated)).astype(jnp.bfloat16)  16.4 us
    concatenate x2, other arithmetic, extended(): value = jnp.concatenate([before, value, after], axis=dim)  10.7 us
  transfers between devices with their start and end apart: 8, of which 5 were waited for; matrix products, arithmetic and copies ran while one was open for 1% of the time, Pallas kernels for 0%

commit v1 on v0

--- a/solution.py
+++ b/solution.py
@@ -1,12 +1,530 @@
+import functools
+
 import jax
 import jax.numpy as jnp
 from jax import lax
+from jax.experimental import pallas as pl
+from jax.experimental.pallas import tpu as pltpu
 from jax.sharding import PartitionSpec as P
 
 CLASSES = 8
-
+LANES = 128
+SUBLANES = 8
+ROWS = 16
+MIB = 1 << 20
 
 shift_value = 0.1
+
+VMEM = pl.BlockSpec(memory_space=pltpu.VMEM)
+SMEM = pl.BlockSpec(memory_space=pltpu.SMEM)
+NT = (((1,), (1,)), ((), ()))
+
+
+def reciprocal(value):
+    guess = pl.reciprocal(value, approx=True)
+    return guess * (2.0 - value * guess)
+
+
+def column_of(row):
+    return jnp.broadcast_to(row, (LANES, LANES)).T
+
+
+def lookup(classes, table):
+    value = jnp.full(classes.shape, table[0], jnp.float32)
+    for index in range(1, CLASSES):
+        value = jnp.where(classes == index, table[index], value)
+    return value
+
+
+def shift_outer(value, axis, step):
+    size = lax.axis_size(axis)
+    return lax.ppermute(value, axis, [(i, (i + 2 * step) % size) for i in range(size)])
+
+
+def swap_inner(value, axis):
+    size = lax.axis_size(axis)
+    return lax.ppermute(value, axis, [(i, i ^ 1) for i in range(size)])
+
+
+def after(value, *given):
+    return lax.optimization_barrier((value, given))[0]
+
+
+def neighbours(first, last, axis):
+    size = lax.axis_size(axis)
+    up = [(i, i + 1) for i in range(size - 1)]
+    down = [(j, i) for i, j in up]
+    return lax.ppermute(last, axis, up), lax.ppermute(first, axis, down)
+
+
+def spread(value, axis):
+    size = lax.axis_size(axis)
+    pieces = {}
+    for step in range(size // 2):
+        kept = value if step == 0 else shift_outer(value, axis, step)
+        pieces[step, 0] = kept
+        pieces[step, 1] = swap_inner(kept, axis)
+    return pieces
+
+
+def owner(index, size, step, swapped):
+    outer = size // 2
+    place = lax.rem(index // 2 + (outer - step), outer)
+    return 2 * place + (1 - lax.rem(index, 2) if swapped else lax.rem(index, 2))
+
+
+def faces_kernel(half_ref, sol_ref, cls_ref, left_ref, right_ref, top_ref, bottom_ref):
+    planes, rows, columns = sol_ref.shape
+    table = [half_ref[i] for i in range(CLASSES)]
+    lane = lax.broadcasted_iota(jnp.int32, (rows, LANES), 1)
+    for ref, place, at in ((left_ref, 0, 0), (right_ref, columns - LANES, LANES - 1)):
+        result = jnp.zeros((rows, LANES), jnp.float32)
+        classes = jnp.zeros((rows, LANES), jnp.int32)
+        for k in range(planes):
+            shift = (k - at) % LANES
+            value = sol_ref[k, :, place : place + LANES]
+            held = cls_ref[k, :, place : place + LANES]
+            if shift:
+                value = pltpu.roll(value, shift, 1)
+            result = jnp.where(lane == k, value, result)
+            shift = (planes + k - at) % LANES
+            if shift:
+                held = pltpu.roll(held, shift, 1)
+            classes = jnp.where(lane == planes + k, held, classes)
+        ref[...] = jnp.where(lane < planes, result, lookup(classes, table))
+    for ref, place in ((top_ref, 0), (bottom_ref, rows - 1)):
+        ref[0] = sol_ref[:, place, :]
+        ref[1] = lookup(cls_ref[:, place, :], table)
+
+
+def cut_kernel(place_ref, matrix_ref, eigen_ref, out_ref):
+    rows, width = matrix_ref.shape[0], out_ref.shape[1]
+    at = pl.multiple_of(place_ref[2] * width, LANES)
+    out_ref[:rows, :] = matrix_ref[:, pl.ds(at, width)]
+    left = eigen_ref[...]
+    row = lax.broadcasted_iota(jnp.int32, (ROWS, rows), 0)
+    result = jnp.zeros((ROWS, rows), jnp.float32)
+    for index in range(3):
+        term = left.astype(jnp.bfloat16).astype(jnp.float32)
+        result = jnp.where(row == index, term, result)
+        left = left - term
+    if width > rows:
+        result = jnp.concatenate([result, jnp.zeros((ROWS, width - rows), jnp.float32)], axis=1)
+    out_ref[rows:, :] = result.astype(jnp.bfloat16)
+
+
+def others_kernel(zs, place_ref, blocks_ref, out_ref):
+    for step in range(1, zs):
+        out_ref[step - 1] = blocks_ref[lax.rem(place_ref[0] + (zs - step), zs)]
+
+
+def stencil_kernel(
+    low,
+    half_ref,
+    wz_ref,
+    sol_ref,
+    cls_ref,
+    src_ref,
+    left_ref,
+    right_ref,
+    top_ref,
+    bottom_ref,
+    wy_ref,
+    wx_ref,
+    out_ref,
+    u_ref,
+    h_ref,
+    sides_ref,
+    wy_col,
+):
+    planes, rows, columns = sol_ref.shape
+    count = out_ref.shape[0]
+    table = [half_ref[i] for i in range(CLASSES)]
+    first, last = max(low - 1, 0), min(low + count, planes - 1)
+    pad = SUBLANES
+    for k in range(first, last + 1):
+        slot = k - first
+        u_ref[slot, pl.ds(pad, rows), :] = sol_ref[k]
+
+        def fill(step, _, k=k, slot=slot):
+            at = pl.multiple_of(step * 2 * SUBLANES, 2 * SUBLANES)
+            h_ref[slot, pl.ds(pad + at, 2 * SUBLANES), :] = lookup(
+                cls_ref[k, pl.ds(at, 2 * SUBLANES), :], table
+            )
+            return 0
+
+        lax.fori_loop(0, rows // (2 * SUBLANES), fill, 0)
+    for k in range(low, low + count):
+        slot = k - first
+        for ref, place, edge in ((top_ref, 0, pad), (bottom_ref, pad + rows, pad + rows - 1)):
+            value, held = ref[0, k : k + 1, :], ref[1, k : k + 1, :]
+            held = jnp.where(held > 0, held, h_ref[slot, edge : edge + 1, :])
+            u_ref[slot, place : place + pad, :] = jnp.broadcast_to(value, (pad, columns))
+            h_ref[slot, place : place + pad, :] = jnp.broadcast_to(held, (pad, columns))
+        lane = lax.broadcasted_iota(jnp.int32, (rows, LANES), 1)
+        for part in range(2):
+            at = part * planes + k
+            before = left_ref[...]
+            after = right_ref[...]
+            before = pltpu.roll(before, (LANES - at) % LANES, 1) if at else before
+            after = pltpu.roll(after, (LANES - 1 - at) % LANES, 1)
+            sides_ref[k - low, part] = jnp.where(lane < LANES // 2, before, after)
+    for block in range(rows // LANES):
+        wy_col[pl.ds(block * LANES, LANES), :] = column_of(
+            wy_ref[:, block * LANES : (block + 1) * LANES]
+        )
+    wx = wx_ref[...]
+    size = 2 * SUBLANES
+    tiles = columns // LANES
+
+    def block(step, _):
+        at = pl.multiple_of(step * size, size)
+        wide = size + 2 * pad
+        lane = lax.broadcasted_iota(jnp.int32, (size, columns), 1)
+        wy = jnp.tile(wy_col[pl.ds(at, size), :], (1, tiles)) * wx
+        below = None
+        if low > 0:
+            below = (u_ref[0, pl.ds(pad + at, size), :], h_ref[0, pl.ds(pad + at, size), :])
+        carried = None
+        for k in range(low, low + count):
+            slot = k - first
+            uw = u_ref[slot, pl.ds(at, wide), :]
+            hw = h_ref[slot, pl.ds(at, wide), :]
+            u, h = uw[pad : pad + size], hw[pad : pad + size]
+            total = (u - pltpu.roll(uw, 1, 0)[pad : pad + size]) * reciprocal(
+                h + pltpu.roll(hw, 1, 0)[pad : pad + size]
+            )
+            total += (u - pltpu.roll(uw, wide - 1, 0)[pad : pad + size]) * reciprocal(
+                h + pltpu.roll(hw, wide - 1, 0)[pad : pad + size]
+            )
+            su = sides_ref[k - low, 0, pl.ds(at, size), :]
+            sh = sides_ref[k - low, 1, pl.ds(at, size), :]
+            if tiles > 1:
+                zeros = jnp.zeros((size, columns - LANES), jnp.float32)
+                su_after = jnp.concatenate([zeros, su], axis=1)
+                sh_after = jnp.concatenate([zeros, sh], axis=1)
+            else:
+                su_after, sh_after = su, sh
+            sh_after = jnp.where(sh_after > 0, sh_after, h)
+            final = lane == columns - 1
+            un = jnp.where(final, su_after, pltpu.roll(u, columns - 1, 1))
+            hn = jnp.where(final, sh_after, pltpu.roll(h, columns - 1, 1))
+            flux = (u - un) * reciprocal(h + hn)
+            u0, h0 = u[:, :LANES], h[:, :LANES]
+            start = (su - u0) * reciprocal(h0 + jnp.where(sh > 0, sh, h0))
+            if tiles > 1:
+                zeros = jnp.zeros((size, columns - LANES), jnp.float32)
+                start = jnp.concatenate([start, zeros], axis=1)
+            total += flux - jnp.where(lane == 0, start, pltpu.roll(flux, 1, 1))
+            if k == 0:
+                total += u * reciprocal(h + h)
+            elif carried is not None:
+                total -= carried
+            else:
+                total += (u - below[0]) * reciprocal(h + below[1])
+            if k == planes - 1:
+                total += u * reciprocal(h + h)
+            else:
+                ua = u_ref[slot + 1, pl.ds(pad + at, size), :]
+                ha = h_ref[slot + 1, pl.ds(pad + at, size), :]
+                carried = (u - ua) * reciprocal(h + ha)
+                total += carried
+            result = (wz_ref[k] * wy) * (src_ref[k, pl.ds(at, size), :] - total)
+            out_ref[k - low, pl.ds(at, size), :] = result.astype(jnp.bfloat16)
+        return 0
+
+    lax.fori_loop(0, rows // size, block, 0)
+
+
+def forward_x_kernel(sizes, names, place_ref, matrix_ref, *refs):
+    bx, zs = sizes
+    pieces, outs, held = refs[: len(names)], refs[len(names) : -1], refs[-1]
+    z, me = place_ref[0], place_ref[2]
+    count, rows, columns = pieces[0].shape
+    part = held.shape[1]
+    for k in range(count):
+        total = None
+        for name, ref in zip(names, pieces):
+            at = pl.multiple_of(owner(me, bx, *name) * columns, LANES)
+            term = lax.dot_general(
+                matrix_ref[:, pl.ds(at, columns)], ref[k], NT, preferred_element_type=jnp.float32
+            )
+            total = term if total is None else total + term
+        for block in range(zs):
+            held[block] = total[block * part : (block + 1) * part].astype(jnp.bfloat16)
+        for step in range(zs):
+            outs[step][k] = held[lax.rem(z + step, zs)]
+
+
+def joined(line, first, count):
+    return jnp.concatenate([line[first + i] for i in range(count)], axis=1)
+
+
+def middle_kernel(
+    sizes, names, chunks, place_ref, fz_ref, iz_ref, ez_ref, ex_ref, ey_ref, own_ref, *refs
+):
+    bx, zs = sizes
+    shares, refs = refs[: len(names)], refs[len(names) :]
+    pieces, refs = refs[: 2 * chunks], refs[2 * chunks :]
+    outs, (line, modes, ex_col) = refs[:chunks], refs[chunks:]
+    z, x, me = place_ref[0], place_ref[1], place_ref[2]
+    count, part, _ = pieces[0].shape
+    planes = count * chunks
+    rows = own_ref.shape[0]
+    quarter = shares[0].shape[2]
+    for chunk in range(chunks):
+        for swapped in range(2):
+            for place in range(zs):
+                block = 2 * place + (1 - x if swapped else x)
+                for k in range(count):
+                    line[block, (chunk * count + k) * part : (chunk * count + k + 1) * part, :] = (
+                        pieces[2 * chunk + swapped][k, :, place * rows : (place + 1) * rows]
+                    )
+    at = pl.multiple_of(z * part, LANES)
+    ex_col[...] = column_of(ex_ref[:, pl.ds(at, part)])
+    tiles = rows // LANES
+    for step in range(zs):
+        if step == 0:
+            total = lax.dot_general(
+                joined(line, 0, 2 * zs), own_ref[...], NT, preferred_element_type=jnp.float32
+            )
+        else:
+            total = None
+            for name, ref in zip(names, shares):
+                term = lax.dot_general(
+                    joined(line, owner(me, bx, *name) * (quarter // rows), quarter // rows),
+                    ref[step - 1, :rows],
+                    NT,
+                    preferred_element_type=jnp.float32,
+                )
+                total = term if total is None else total + term
+        modes[...] = total
+        ey = ey_ref[...]
+        if step > 0:
+            ey = jnp.sum(shares[0][step - 1, rows:, :rows].astype(jnp.float32), 0, keepdims=True)
+        ey += shift_value
+
+        def mix(at, _, step=step, ey=ey):
+            at = pl.multiple_of(at * ROWS, ROWS)
+            ex = jnp.tile(ex_col[pl.ds(at, ROWS), :], (1, tiles)) + ey
+            given = [modes[pl.ds(k * part + at, ROWS), :] for k in range(planes)]
+            scaled = []
+            for q in range(planes):
+                value = fz_ref[q, 0] * given[0]
+                for k in range(1, planes):
+                    value += fz_ref[q, k] * given[k]
+                scaled.append(value * reciprocal(ex + ez_ref[q]))
+            for k in range(planes):
+                value = iz_ref[k, 0] * scaled[0]
+                for q in range(1, planes):
+                    value += iz_ref[k, q] * scaled[q]
+                outs[k // count][k % count, pl.ds(at, ROWS), step * rows : (step + 1) * rows] = (
+                    value.astype(jnp.bfloat16)
+                )
+            return 0
+
+        lax.fori_loop(0, part // ROWS, mix, 0)
+
+
+def inverse_y_kernel(sizes, names, place_ref, own_ref, *refs):
+    bx, zs = sizes
+    shares, refs = refs[: len(names)], refs[len(names) :]
+    spectra, outs, line = refs[:2], refs[2:-1], refs[-1]
+    z, x, me = place_ref[0], place_ref[1], place_ref[2]
+    count, part, _ = spectra[0].shape
+    rows = own_ref.shape[0]
+    quarter = shares[0].shape[2]
+    for swapped in range(2):
+        for step in range(zs):
+            block = 2 * lax.rem(z + (zs - step), zs) + (1 - x if swapped else x)
+            for k in range(count):
+                line[block, k * part : (k + 1) * part, :] = spectra[swapped][
+                    k, :, step * rows : (step + 1) * rows
+                ]
+    for step in range(zs):
+        if step == 0:
+            total = lax.dot_general(
+                own_ref[...], joined(line, 0, 2 * zs), NT, preferred_element_type=jnp.float32
+            )
+        else:
+            total = None
+            for name, ref in zip(names, shares):
+                term = lax.dot_general(
+                    ref[zs - step - 1, :rows],
+                    joined(line, owner(me, bx, *name) * (quarter // rows), quarter // rows),
+                    NT,
+                    preferred_element_type=jnp.float32,
+                )
+                total = term if total is None else total + term
+        for k in range(count):
+            outs[step][k] = total[:, k * part : (k + 1) * part].astype(jnp.bfloat16)
+
+
+def merge_kernel(zs, place_ref, *refs):
+    pieces, out = refs[:-1], refs[-1]
+    part = pieces[0].shape[2]
+    for step, ref in enumerate(pieces):
+        at = pl.multiple_of(lax.rem(place_ref[0] + (zs - step), zs) * part, LANES)
+        out[:, :, pl.ds(at, part)] = ref[...]
+
+
+def inverse_x_kernel(bx, names, low, place_ref, wz_ref, wy_ref, wx_ref, sol_ref, matrix_ref, *refs):
+    pieces, out_ref, wy_col = refs[: len(names)], refs[-2], refs[-1]
+    me = place_ref[2]
+    k = pl.program_id(0)
+    rows, columns = out_ref.shape[1:]
+    width = pieces[0].shape[2]
+    for block in range(rows // LANES):
+        wy_col[pl.ds(block * LANES, LANES), :] = column_of(
+            wy_ref[:, block * LANES : (block + 1) * LANES]
+        )
+    total = None
+    for name, ref in zip(names, pieces):
+        at = pl.multiple_of(owner(me, bx, *name) * width, LANES)
+        term = lax.dot_general(
+            ref[k], matrix_ref[:, pl.ds(at, width)], NT, preferred_element_type=jnp.float32
+        )
+        total = term if total is None else total + term
+    weight = wz_ref[low + k] * (jnp.tile(wy_col[...], (1, columns // LANES)) * wx_ref[...])
+    out_ref[0] = sol_ref[0] + weight * total
+
+
+def params(mib):
+    return pltpu.CompilerParams(vmem_limit_bytes=mib * MIB)
+
+
+def cost(flops, nbytes):
+    return pl.CostEstimate(flops=flops // 16, bytes_accessed=nbytes // 16, transcendentals=0)
+
+
+def on_device_tiled(
+    solution,
+    source,
+    class_ids,
+    conductivity,
+    spacing_x,
+    spacing_y,
+    spacing_z,
+    forward_x,
+    forward_y,
+    forward_z,
+    inverse_x,
+    inverse_y,
+    inverse_z,
+    eigen_x,
+    eigen_y,
+    eigen_z,
+):
+    f32, bf16 = jnp.float32, jnp.bfloat16
+    bx, by = lax.axis_size("bx"), lax.axis_size("by")
+    zs = by // 2
+    sizes = (bx, zs)
+    planes, rows, columns = solution.shape
+    part = columns // zs
+    length = forward_y.shape[1]
+    chunks = 2 if planes % 2 == 0 else 1
+    count = planes // chunks
+    at_x, at_y = lax.axis_index("bx"), lax.axis_index("by")
+    place = jnp.stack([at_y // 2, at_y % 2, at_x]).astype(jnp.int32)
+    half = 0.5 / conductivity
+    fz, iz = forward_z.astype(f32), inverse_z.astype(f32)
+    wx, wy = spacing_x.reshape(1, -1), spacing_y.reshape(1, -1)
+
+    quarter = length // bx
+
+    def cut(matrix, eigen):
+        mine = pl.pallas_call(
+            cut_kernel,
+            out_shape=jax.ShapeDtypeStruct((rows + ROWS, quarter), bf16),
+            in_specs=[SMEM, VMEM, VMEM],
+            out_specs=VMEM,
+            compiler_params=params(4),
+            cost_estimate=cost(1 << 20, 1 << 20),
+            name="cut",
+        )(place, matrix, eigen)
+        groups = [[2 * i + j for i in range(zs)] for j in range(2)]
+        return lax.all_gather(mine, "by", axis_index_groups=groups)
+
+    def others(gathered):
+        return pl.pallas_call(
+            functools.partial(others_kernel, zs),
+            out_shape=jax.ShapeDtypeStruct((zs - 1, rows + ROWS, quarter), bf16),
+            in_specs=[SMEM, VMEM],
+            out_specs=VMEM,
+            compiler_params=params(4),
+            cost_estimate=cost(1 << 20, 1 << 20),
+            name="others",
+        )(place, gathered)
+
+    def merge(pieces):
+        count, rows, width = pieces[0].shape
+        return pl.pallas_call(
+            functools.partial(merge_kernel, zs),
+            out_shape=jax.ShapeDtypeStruct((count, rows, zs * width), bf16),
+            in_specs=[SMEM] + [VMEM] * zs,
+            out_specs=VMEM,
+            compiler_params=params(8),
+            cost_estimate=cost(1 << 20, 1 << 20),
+            name="merge",
+        )(place, *pieces)
+
+    def exchange(pieces):
+        return merge(
+            [
+                piece if step == 0 else shift_outer(piece, "by", step)
+                for step, piece in enumerate(pieces)
+            ]
+        )
+
+    left, right, top, bottom = pl.pallas_call(
+        faces_kernel,
+        out_shape=(
+            jax.ShapeDtypeStruct((rows, LANES), f32),
+            jax.ShapeDtypeStruct((rows, LANES), f32),
+            jax.ShapeDtypeStruct((2, planes, columns), f32),
+            jax.ShapeDtypeStruct((2, planes, columns), f32),
+        ),
+        in_specs=[SMEM, VMEM, VMEM],
+        out_specs=[VMEM] * 4,
+        compiler_params=params(12),
+        cost_estimate=cost(1 << 20, 1 << 20),
+        name="faces",
+    )(half, solution, class_ids)
+    left, right = neighbours(left, right, "bx")
+    top, bottom = neighbours(top, bottom, "by")
+
+    ey = eigen_y.reshape(1, -1)
+    names = tuple((step, swapped) for step in range(bx // 2) for swapped in range(2))
+
+    gathered = []
+    for chunk in range(chunks):
+        low = chunk * count
+        held = min(low + count, planes - 1) - max(low - 1, 0) + 1
+        restricted = pl.pallas_call(
+            functools.partial(stencil_kernel, low),
+            out_shape=jax.ShapeDtypeStruct((count, rows, columns), bf16),
+            in_specs=[SMEM, SMEM] + [VMEM] * 9,
+            out_specs=VMEM,
+            scratch_shapes=[
+                pltpu.VMEM((held, rows + 2 * SUBLANES, columns), f32),
+                pltpu.VMEM((held, rows + 2 * SUBLANES, columns), f32),
+                pltpu.VMEM((count, 2, rows, LANES), f32),
+                pltpu.VMEM((rows, LANES), f32),
+            ],
+            compiler_params=params(24),
+            cost_estimate=cost(1 << 26, 8 << 20),
+            name="stencil",
+        )(half, spacing_z, solution, class_ids, source, left, right, top, bottom, wy, wx)
+        gathered.append(restricted)
+    highest = lax.Precision.HIGHEST
+    restricted = jnp.concatenate(gathered, axis=0)
+    weights = spacing_z[:, None, None] * spacing_y[None, :, None] * spacing_x[None, None, :]
+    modes_xy = x_high(y_low(restricted, forward_y), forward_x)
+    modes = jnp.einsum("qk,knm->qnm", fz, modes_xy, precision=highest)
+    divisor = eigen_x[None, None, :] + eigen_y[None, :, None] + eigen_z[:, None, None] + shift_value
+    spectral = jnp.einsum("kq,qnm->knm", iz, modes / divisor, precision=highest).astype(bf16)
+    field = x_high(y_low(spectral, inverse_y), inverse_x)
+    return solution + weights * field
 
 
 def extended(value, sides, width):
@@ -71,7 +589,7 @@
     )
 
 
-def on_device(
+def on_device_plain(
     solution,
     source,
     class_ids,
@@ -105,6 +623,15 @@
     return solution + weights * field
 
 
+def tiled(mesh, shape):
+    bx, by = mesh.shape["bx"], mesh.shape["by"]
+    planes, rows, columns = shape
+    rows, columns = rows // by, columns // bx
+    if bx % 2 or by % 2 or rows % LANES or columns % (LANES * (by // 2)):
+        return False
+    return (2 * planes) <= LANES and columns // (by // 2) == LANES and by % bx == 0
+
+
 def solution(mesh):
     in_specs = (
         P(None, "by", "bx"),
@@ -125,6 +652,11 @@
         P(),
     )
     out_specs = P(None, "by", "bx")
-    return jax.shard_map(
-        on_device, mesh=mesh, in_specs=in_specs, out_specs=out_specs, check_vma=False
-    )
+
+    def whole(*operands):
+        body = on_device_tiled if tiled(mesh, operands[0].shape) else on_device_plain
+        return jax.shard_map(
+            body, mesh=mesh, in_specs=in_specs, out_specs=out_specs, check_vma=False
+        )(*operands)
+
+    return whole

time: 510 us -> 470 us (0.922)
  other arithmetic: 35.5 us -> 2.04 us
  local copies, waits for them, and re-layouts: 30.3 us -> 5.44 us
  Pallas kernels: 0 us -> 11.9 us
  matrix products: 51.3 us -> 57.2 us
    convert_element_type x1 -> x0, other arithmetic: 16.4 us -> none  [on_device(): restricted = (weights * (source - operated)).astype(jnp.bfloat16)]
    pallas_call x0 -> x3, Pallas kernels: none -> 11.9 us  [the longest x2 10.7 us: on_device_tiled(): pl.pallas_call(functools.partial(stencil_kernel, low), out_shape=jax.Shap...]
    concatenate x2 -> x1, other arithmetic: 10.7 us -> 1.06 us  [on_device_tiled(): restricted = jnp.concatenate(gathered, axis=0)]
    slice x6 -> x0, local copies, waits for them, and re-layouts: 8.99 us -> none  [the longest x3 5.03 us: extended(): last = lax.slice_in_dim(value, length - width, length, axis=dim)]
    another operation x1 -> x0, other arithmetic: 8.15 us -> none  [operate(): stacked = jnp.stack([solution, coef])]
    dot_general x2, matrix products: 27.2 us -> 33.4 us  [x_high(): jnp.einsum('kjx,mx->kjm', lax.all_gather(values, 'bx', axis=2, tiled=True...]
  transfers between devices with their start and end apart: 8 -> 8, of which waited for: 5 -> 6; matrix products, arithmetic and copies ran while one was open for 1% -> 0% of each run, Pallas kernels for 0% -> 0%
where the time goes in v1:
time: 470 us
  waiting for transfers between devices  371 us (79%)
  matrix products  57.2 us (12%)
  between operations  13.3 us (3%)
  Pallas kernels  11.9 us (3%)
  starting transfers between devices  9.43 us (2%)
  local copies, waits for them, and re-layouts  5.44 us (1%)
    all_gather x2, waiting for transfers between devices, y_low(): lax.all_gather(values, 'by', axis=1, tiled=True)  254 us
    all_gather x2, waiting for transfers between devices, x_high(): lax.all_gather(values, 'bx', axis=2, tiled=True)  112 us
    dot_general x2, matrix products, x_high(): jnp.einsum('kjx,mx->kjm', lax.all_gather(values, 'bx', axis=2, tiled=True...  33.4 us
    dot_general x2, matrix products, y_low(): jnp.einsum('kjm,nj->knm', lax.all_gather(values, 'by', axis=1, tiled=True...  16.7 us
    pallas_call x2, Pallas kernels, on_device_tiled(): pl.pallas_call(functools.partial(stencil_kernel, low), out_shape=jax.Shap...  10.7 us
  transfers between devices with their start and end apart: 8, of which 6 were waited for; matrix products, arithmetic and copies ran while one was open for 0% of the time, Pallas kernels for 0%

profile of v1, /device:TPU:0, one launch (start us, length us, event | category | flops | bytes accessed | tf_op | source)
XLA Modules:
  0.0 470.0 jit_solution(4913602643877789287)
XLA Ops:
  6.5 0.0 copy-start
  6.5 0.0 all-gather.5.cloned.1.call-start
  6.5 0.8 broadcast_divide_fusion.half_ref
  7.3 0.0 copy-start.1
  7.3 1.6 copy-done.1
  8.9 0.0 copy-start.3
  8.9 1.6 copy-done.3
  10.5 0.0 copy-start.2
  10.5 0.0 copy-start.4
  10.5 0.0 copy-start.6
  10.5 0.0 copy-start.7
  10.5 0.0 copy-start.8
  10.6 1.2 faces.1
  11.8 2.5 collective-permute-start
  14.3 1.3 collective-permute-start.1
  15.6 4.2 collective-permute-start.2
  19.8 1.3 collective-permute-start.3
  21.1 0.1 collective-permute-done.2.top_ref
  21.3 4.2 collective-permute-done.3.bottom_ref
  25.5 0.0 collective-permute-done.left_ref
  25.5 0.0 collective-permute-done.1.right_ref
  25.5 0.0 copy-done.2
  25.5 0.0 copy-done.4
  25.5 0.0 copy-done.6
  25.5 0.0 copy-done.7
  25.5 0.0 copy-done.8
  25.5 0.0 copy-start.5
  25.5 1.6 copy-done.5
  27.1 5.3 %stencil.2 = bf16[2,256,512]{2,1,0:T(8,128)(2,1)S(1)} custom-call(f32[8]{0:T(128)S(1)} %broadcast_divide_fusion.half_ref, f32[4]{0:T(128)S(1)} %copy-done.8, f32[4,256,512]{2,1,0:T(8,128)S(1)} %copy-done.4, s32[4,256,512]{2,1,0:T(8,128)S(1)} %copy-done.2, f32[4,256,512]{2,1,0:T(8,128)S(1)} %copy-done.5, f32[256,128]{1,0:T(8,128)S(1)} %collective-permute-done.left_ref, ...), custom_call_target="tpu_custom_call" | custom-call | flops 4194304 | bytes 524288 | tf_op jit(solution)/shard_map/stencil/pallas_call | solution.py:503
  32.5 5.4 %stencil.3 = bf16[2,256,512]{2,1,0:T(8,128)(2,1)S(1)} custom-call(f32[8]{0:T(128)S(1)} %broadcast_divide_fusion.half_ref, f32[4]{0:T(128)S(1)} %copy-done.8, f32[4,256,512]{2,1,0:T(8,128)S(1)} %copy-done.4, s32[4,256,512]{2,1,0:T(8,128)S(1)} %copy-done.2, f32[4,256,512]{2,1,0:T(8,128)S(1)} %copy-done.5, f32[256,128]{1,0:T(8,128)S(1)} %collective-permute-done.left_ref, ...), custom_call_target="tpu_custom_call" | custom-call | flops 4194304 | bytes 524288 | tf_op jit(solution)/shard_map/stencil/pallas_call | solution.py:503
  37.8 0.0 copy-start.12
  37.9 1.1 pad_maximum_fusion
  38.9 0.0 all-gather.5.cloned.1.call-update
  38.9 0.0 all-gather.7.cloned.1.call-start
  39.0 128.7 %all-gather.5.cloned.1.call-done = bf16[4,2048,512]{2,1,0:T(8,128)(2,1)} async-done(((bf16[4,256,512]{2,1,0:T(8,128)(2,1)}), bf16[4,2048,512]{2,1,0:T(8,128)(2,1)}) %all-gather.5.cloned.1.call-update) | async-done | bytes 8388624 | tf_op jit(solution)/shard_map/all_gather | solution.py:586
  167.7 0.0 copy-done.12
  167.7 7.1 %convolution_bitcast_fusion = f32[4,256,512]{1,2,0:T(8,128)} fusion(bf16[4,2048,512]{2,1,0:T(8,128)(2,1)} %all-gather.5.cloned.1.call-done, bf16[256,2048]{1,0:T(8,128)(2,1)S(1)} %copy-done.12), kind=kOutput, calls=%fused_computation.12 | convolution fusion | flops 2147483648 | bytes 11534336 | tf_op jit(solution)/shard_map/kjm,nj->knm/dot_general | solution.py:584
  174.9 0.0 copy-start.9
  174.9 0.0 copy-start.10
  174.9 0.0 all-gather.7.cloned.1.call-update
  174.9 0.0 all-gather.9.cloned.1.call-start
  174.9 0.6 copy-done.9
  175.6 0.0 copy-done.10
  175.6 0.1 broadcast_add_fusion
  175.7 0.0 copy-start.11
  175.7 55.8 %all-gather.7.cloned.1.call-done = f32[4,256,2048]{1,2,0:T(8,128)} async-done(((f32[4,256,512]{1,2,0:T(8,128)}), f32[4,256,2048]{1,2,0:T(8,128)}) %all-gather.7.cloned.1.call-update) | async-done | bytes 8388624 | tf_op jit(solution)/shard_map/all_gather | solution.py:577
  231.5 0.0 copy-done
  231.5 15.8 %fusion.4 = f32[4,256,512]{2,1,0:T(8,128)S(1)} fusion(f32[4,256,2048]{1,2,0:T(8,128)} %all-gather.7.cloned.1.call-done, bf16[512,2048]{1,0:T(8,128)(2,1)S(1)} %copy-done), kind=kOutput, calls=%fused_computation.5 | convolution fusion | flops 12884901888 | bytes 12582912 | tf_op jit(solution)/shard_map/kjx,mx->kjm/dot_general | solution.py:575
  247.4 0.0 copy-done.11
  247.4 0.0 copy-start.13
  247.4 0.0 copy-start.14
  247.4 3.2 fusion.6
  250.6 0.0 copy-done.13
  250.6 0.0 copy-done.14
  250.6 3.9 fusion.15
  254.5 0.0 all-gather.9.cloned.1.call-update
  254.6 0.0 all-gather.11.cloned.1.call-start
  254.6 125.0 %all-gather.9.cloned.1.call-done = bf16[4,2048,512]{2,0,1:T(4,128)(2,1)} async-done(((bf16[4,256,512]{2,0,1:T(4,128)(2,1)}), bf16[4,2048,512]{2,0,1:T(4,128)(2,1)}) %all-gather.9.cloned.1.call-update) | async-done | bytes 8388624 | tf_op jit(solution)/shard_map/all_gather | solution.py:586
  379.6 9.6 %fusion.11 = f32[4,256,512]{1,2,0:T(8,128)} fusion(bf16[4,2048,512]{2,0,1:T(4,128)(2,1)} %all-gather.9.cloned.1.call-done, bf16[256,2048]{1,0:T(8,128)(2,1)} %param.27), kind=kOutput, calls=%fused_computation.11 | convolution fusion | flops 2147483648 | bytes 11534336 | tf_op jit(solution)/shard_map/kjm,nj->knm/dot_general | solution.py:584
  389.2 0.0 all-gather.11.cloned.1.call-update
  389.2 0.1 broadcast_multiply_fusion
  389.3 56.6 %all-gather.11.cloned.1.call-done = f32[4,256,2048]{1,2,0:T(8,128)} async-done(((f32[4,256,512]{1,2,0:T(8,128)}), f32[4,256,2048]{1,2,0:T(8,128)}) %all-gather.11.cloned.1.call-update) | async-done | bytes 8388624 | tf_op jit(solution)/shard_map/all_gather | solution.py:577
  445.9 17.6 %multiply_add_fusion = f32[4,256,512]{2,1,0:T(8,128)} fusion(f32[4,256,512]{2,1,0:T(8,128)} %sol_ref.5, f32[4,256,2048]{1,2,0:T(8,128)} %all-gather.11.cloned.1.call-done, bf16[512,2048]{1,0:T(8,128)(2,1)} %param.26, f32[512]{0:T(512)S(1)} %copy-done.7, f32[4,256]{1,0:T(4,128)S(1)} %broadcast_multiply_fusion), kind=kOutput, calls=%fused_computation.9 | convolution fusion | flops 12886474752 | bytes 14686208 | tf_op jit(solution)/shard_map/kjx,mx->kjm/dot_general | solution.py:575
Async XLA Ops:
  6.5 225.0 %copy-start = (bf16[512,2048]{1,0:T(8,128)(2,1)S(1)}, bf16[512,2048]{1,0:T(8,128)(2,1)}, u32[]{:S(2)}) copy-start(bf16[512,2048]{1,0:T(8,128)(2,1)} %param.23) | copy-start | bytes 6291460
  6.5 161.2 %all-gather.5.cloned.1.call-start = ((), (), s32[]{:S(2)}) async-start(), calls=%async_computation | async-start | bytes 9437184 | tf_op jit(solution)/shard_map/all_gather | solution.py:586
  7.3 1.6 copy-start.1
  8.9 1.6 copy-start.3
  10.5 14.9 %copy-start.2 = (s32[4,256,512]{2,1,0:T(8,128)S(1)}, s32[4,256,512]{2,1,0:T(8,128)}, u32[]{:S(2)}) copy-start(s32[4,256,512]{2,1,0:T(8,128)} %cls_ref.5) | copy-start | bytes 6291460
  10.5 14.9 %copy-start.4 = (f32[4,256,512]{2,1,0:T(8,128)S(1)}, f32[4,256,512]{2,1,0:T(8,128)}, u32[]{:S(2)}) copy-start(f32[4,256,512]{2,1,0:T(8,128)} %sol_ref.5) | copy-start | bytes 6291460
  10.5 14.9 %copy-start.6 = (f32[256]{0:T(256)S(1)}, f32[256]{0:T(256)}, u32[]{:S(2)}) copy-start(f32[256]{0:T(256)} %param.21) | copy-start | bytes 3076
  10.5 15.0 %copy-start.7 = (f32[512]{0:T(512)S(1)}, f32[512]{0:T(512)}, u32[]{:S(2)}) copy-start(f32[512]{0:T(512)} %param.20) | copy-start | bytes 6148
  10.5 15.0 %copy-start.8 = (f32[4]{0:T(128)S(1)}, f32[4]{0:T(128)}, u32[]{:S(2)}) copy-start(f32[4]{0:T(128)} %wz_ref.3) | copy-start | bytes 52
  11.8 13.7 %collective-permute-start = (f32[256,128]{1,0:T(8,128)S(1)}, f32[256,128]{1,0:T(8,128)S(1)}, u32[]{:S(2)}, u32[]{:S(2)}) collective-permute-start(f32[256,128]{1,0:T(8,128)S(1)} %get-tuple-element.9), channel_id=1, source_target_pairs={{0,8},{8,16},{16,24},{1,9},{9,17},{17,25},{2,10},{10,18},{18,26},{... | collective-permute-start | bytes 393224 | tf_op jit(solution)/shard_map/ppermute | solution.py:57
  14.3 11.2 %collective-permute-start.1 = (f32[256,128]{1,0:T(8,128)S(1)}, f32[256,128]{1,0:T(8,128)S(1)}, u32[]{:S(2)}, u32[]{:S(2)}) collective-permute-start(f32[256,128]{1,0:T(8,128)S(1)} %get-tuple-element.10), channel_id=1, source_target_pairs={{8,0},{16,8},{24,16},{9,1},{17,9},{25,17},{10,2},{18,10},{26,18},{... | collective-permute-start | bytes 393224 | tf_op jit(solution)/shard_map/ppermute | solution.py:57
  15.6 5.7 %collective-permute-start.2 = (f32[2,4,512]{2,1,0:T(4,128)S(1)}, f32[2,4,512]{2,1,0:T(4,128)S(1)}, u32[]{:S(2)}, u32[]{:S(2)}) collective-permute-start(f32[2,4,512]{2,1,0:T(4,128)S(1)} %get-tuple-element.11), channel_id=1, source_target_pairs={{0,1},{1,2},{2,3},{3,4},{4,5},{5,6},{6,7},{8,9},{9,10},{10,11},{11... | collective-permute-start | bytes 49160 | tf_op jit(solution)/shard_map/ppermute | solution.py:57
  19.8 5.6 %collective-permute-start.3 = (f32[2,4,512]{2,1,0:T(4,128)S(1)}, f32[2,4,512]{2,1,0:T(4,128)S(1)}, u32[]{:S(2)}, u32[]{:S(2)}) collective-permute-start(f32[2,4,512]{2,1,0:T(4,128)S(1)} %get-tuple-element.12), channel_id=1, source_target_pairs={{1,0},{2,1},{3,2},{4,3},{5,4},{6,5},{7,6},{9,8},{10,9},{11,10},{12... | collective-permute-start | bytes 49160 | tf_op jit(solution)/shard_map/ppermute | solution.py:57
  25.5 1.6 copy-start.5
  37.8 129.9 %copy-start.12 = (bf16[256,2048]{1,0:T(8,128)(2,1)S(1)}, bf16[256,2048]{1,0:T(8,128)(2,1)}, u32[]{:S(2)}) copy-start(bf16[256,2048]{1,0:T(8,128)(2,1)} %param.24) | copy-start | bytes 3145732
  38.9 192.6 %all-gather.7.cloned.1.call-start = ((), (), s32[]{:S(2)}) async-start(), calls=%async_computation.1 | async-start | bytes 10485760 | tf_op jit(solution)/shard_map/all_gather | solution.py:577
  174.9 0.7 copy-start.9
  174.9 0.7 copy-start.10
  174.9 204.7 %all-gather.9.cloned.1.call-start = ((), (), s32[]{:S(2)}) async-start(), calls=%async_computation.2 | async-start | bytes 9437184 | tf_op jit(solution)/shard_map/all_gather | solution.py:586
  175.7 71.7 %copy-start.11 = (bf16[4,4]{1,0:T(4,128)(2,1)S(1)}, bf16[4,4]{1,0:T(4,128)(2,1)}, u32[]{:S(2)}) copy-start(bf16[4,4]{1,0:T(4,128)(2,1)} %param.25) | copy-start | bytes 100
  247.4 3.3 copy-start.13
  247.4 3.3 copy-start.14
  254.6 191.3 %all-gather.11.cloned.1.call-start = ((), (), s32[]{:S(2)}) async-start(), calls=%async_computation.3 | async-start | bytes 10485760 | tf_op jit(solution)/shard_map/all_gather | solution.py:577
Sparse Core Ops, SparseCore 0:
  39.1 128.6 all-gather.4
  175.0 56.4 all-gather.6
  254.7 124.9 all-gather.8
  389.3 56.4 all-gather.10
